TPU v7x, 32 devices: a whole 2x2x4 slice. The times are simulated.
32 devices in a mesh: node: 8 (over y, x, core), local: 4 (over z).
Axes of the slice: x: 2, y: 2, z: 4, core: 2. Of those that a mesh axis runs over, the one named last changes fastest.
Arguments:
- tokens: bfloat16 [8192, 3072], P(('node', 'local')), may hold values from -6 to 6
- out_grad: bfloat16 [8192, 512], P(('node', 'local')), may hold values from -6 to 6
- weights: bfloat16 [3072, 512], P(('node', 'local')), may hold values from -0.109375 to 0.109375
Outputs:
- projected: bfloat16 [8192, 512], P(('node', 'local'))
- input_grad: bfloat16 [8192, 3072], P(('node', 'local'))
- weight_grad: bfloat16 [3072, 512], P(('node', 'local'))
All inputs are finite; a program needn't handle non-finite values.
Results may differ from a plain program's by a relative error of at most 0.005.
Values may be sent and summed in bfloat16 or wider, within the bound.
A program may use at most 64 MiB of HBM per device.

v0:
```python
import jax
import jax.numpy as jnp
from jax import lax
from jax.sharding import PartitionSpec as P


def per_device(tokens, out_grad, weights):
    tok_rows = tokens.shape[0]
    node_count = lax.axis_size("node")
    local_count = lax.axis_size("local")
    grad_scale = 1.0 / jnp.sqrt(jnp.float32(tok_rows * node_count * local_count))
    contract_rows = (((0,), (0,)), ((), ()))
    contract_cols = (((1,), (1,)), ((), ()))
    grad_term = lax.dot_general(tokens, out_grad, contract_rows, preferred_element_type=jnp.float32)
    grad_term = (grad_term * grad_scale).astype(jnp.bfloat16)
    grad_term = lax.optimization_barrier(grad_term).astype(jnp.float32)
    shard_rows = lax.all_gather(weights, ("node", "local"), axis=0, tiled=True)
    keys_acc = jnp.dot(tokens, shard_rows, preferred_element_type=jnp.float32)
    grad_cols = lax.dot_general(
        out_grad, shard_rows, contract_cols, preferred_element_type=jnp.float32
    )
    grad_acc = grad_cols
    keys_acc, grad_acc = (keys_acc, grad_acc)
    projected = keys_acc.astype(jnp.bfloat16)
    input_grad = grad_acc.astype(jnp.bfloat16)
    across = lax.psum_scatter(grad_term, "node", scatter_dimension=0, tiled=True)
    summed = lax.psum_scatter(across, "local", scatter_dimension=0, tiled=True)
    weight_grad = summed.astype(jnp.bfloat16)
    return (projected, input_grad, weight_grad)


def solution(mesh):
    return jax.shard_map(
        per_device,
        mesh=mesh,
        in_specs=(
            P(("node", "local"), None),
            P(("node", "local"), None),
            P(("node", "local"), None),
        ),
        out_specs=(
            P(("node", "local"), None),
            P(("node", "local"), None),
            P(("node", "local"), None),
        ),
        check_vma=False,
    )
```

profile of v0, /device:TPU:0, one launch (start us, length us, event | category | flops | bytes accessed | tf_op | source)
XLA Modules:
  0.0 114.8 jit_solution(12637521152094354999)
XLA Ops:
  8.0 0.0 copy-start
  8.0 0.0 reduce-scatter.3.cloned.1.call-start
  8.1 1.4 %copy-done = bf16[256,3072]{1,0:T(8,128)(2,1)S(1)} copy-done((bf16[256,3072]{1,0:T(8,128)(2,1)S(1)}, bf16[256,3072]{1,0:T(8,128)(2,1)}, u32[]{:S(2)}) %copy-start) | copy-done | bytes 1572888
  9.4 2.0 %multiply_convert_fusion = bf16[3072,512]{1,0:T(8,128)(2,1)S(1)} fusion(bf16[256,3072]{1,0:T(8,128)(2,1)S(1)} %copy-done, bf16[256,512]{1,0:T(8,128)(2,1)} %param.4), kind=kOutput, calls=%fused_computation | convolution fusion | flops 808452096 | bytes 4980736 | tf_op jit(solution)/shard_map/dot_general | solution.py:14
  11.4 3.6 %convert_element_type.18 = f32[3072,512]{1,0:T(8,128)} convert(bf16[3072,512]{1,0:T(8,128)(2,1)S(1)} %multiply_convert_fusion) | non-fusion elementwise | flops 1572864 | bytes 9437184 | tf_op jit(solution)/shard_map/convert_element_type | solution.py:16
  14.9 0.0 copy-start.2
  14.9 0.0 reduce-scatter.3.cloned.1.call-update
  15.0 0.0 all-gather.2.cloned.1.call-start
  15.0 0.5 all-gather.2.cloned.1.call-update
  15.5 0.0 reduce-scatter.5.cloned.1.call-start
  15.6 64.4 %reduce-scatter.3.cloned.1.call-done = f32[384,512]{1,0:T(8,128)} async-done(((f32[3072,512]{1,0:T(8,128)}), f32[384,512]{1,0:T(8,128)}) %reduce-scatter.3.cloned.1.call-update) | async-done | bytes 786448 | tf_op jit(solution)/shard_map/reduce_scatter | solution.py:26
  80.0 0.0 reduce-scatter.5.cloned.1.call-update
  80.0 14.0 %all-gather.2.cloned.1.call-done = bf16[3072,512]{1,0:T(8,128)(2,1)} async-done(((bf16[96,512]{1,0:T(8,128)(2,1)}), bf16[3072,512]{1,0:T(8,128)(2,1)}) %all-gather.2.cloned.1.call-update) | async-done | bytes 3145744 | tf_op jit(solution)/shard_map/all_gather | solution.py:17
  94.0 0.0 copy-done.2
  94.0 0.0 copy-start.1
  94.0 4.2 %convolution_convert_fusion = bf16[256,3072]{1,0:T(8,128)(2,1)} fusion(bf16[256,512]{1,0:T(8,128)(2,1)S(1)} %copy-done.2, bf16[3072,512]{1,0:T(8,128)(2,1)} %all-gather.2.cloned.1.call-done), kind=kOutput, calls=%fused_computation.1 | convolution fusion | flops 806092800 | bytes 4980736 | tf_op jit(solution)/shard_map/dot_general | solution.py:19
  98.2 0.0 copy-done.1
  98.2 1.7 %convolution_convert_fusion.1 = bf16[256,512]{1,0:T(8,128)(2,1)} fusion(bf16[256,3072]{1,0:T(8,128)(2,1)S(1)} %copy-done, bf16[3072,512]{1,0:T(8,128)(2,1)S(1)} %copy-done.1), kind=kOutput, calls=%fused_computation.2 | convolution fusion | flops 805437440 | bytes 4980736 | tf_op jit(solution)/shard_map/dot_general | solution.py:18
  100.0 5.8 %reduce-scatter.5.cloned.1.call-done = f32[96,512]{1,0:T(8,128)} async-done(((f32[384,512]{1,0:T(8,128)}), f32[96,512]{1,0:T(8,128)}) %reduce-scatter.5.cloned.1.call-update) | async-done | bytes 196624 | tf_op jit(solution)/shard_map/reduce_scatter | solution.py:27
  105.8 1.6 %convert_element_type.19 = bf16[96,512]{1,0:T(8,128)(2,1)} convert(f32[96,512]{1,0:T(8,128)} %reduce-scatter.5.cloned.1.call-done) | non-fusion elementwise | flops 49152 | bytes 294912 | tf_op jit(solution)/shard_map/convert_element_type | solution.py:28
Async XLA Ops:
  8.0 1.4 %copy-start = (bf16[256,3072]{1,0:T(8,128)(2,1)S(1)}, bf16[256,3072]{1,0:T(8,128)(2,1)}, u32[]{:S(2)}) copy-start(bf16[256,3072]{1,0:T(8,128)(2,1)} %param.3) | copy-start | bytes 4718596
  8.0 72.0 %reduce-scatter.3.cloned.1.call-start = ((), (), s32[]{:S(2)}) async-start(), calls=%async_computation.3 | async-start | bytes 7077888 | tf_op jit(solution)/shard_map/reduce_scatter | solution.py:26
  14.9 79.1 %copy-start.2 = (bf16[256,512]{1,0:T(8,128)(2,1)S(1)}, bf16[256,512]{1,0:T(8,128)(2,1)}, u32[]{:S(2)}) copy-start(bf16[256,512]{1,0:T(8,128)(2,1)} %param.4) | copy-start | bytes 786436
  15.0 79.0 %all-gather.2.cloned.1.call-start = ((), (), s32[]{:S(2)}) async-start(), calls=%async_computation.2 | async-start | bytes 3244032 | tf_op jit(solution)/shard_map/all_gather | solution.py:17
  15.5 90.2 %reduce-scatter.5.cloned.1.call-start = ((), (), s32[]{:S(2)}) async-start(), calls=%async_computation.4 | async-start | bytes 983040 | tf_op jit(solution)/shard_map/reduce_scatter | solution.py:27
  94.0 4.2 %copy-start.1 = (bf16[3072,512]{1,0:T(8,128)(2,1)S(1)}, bf16[3072,512]{1,0:T(8,128)(2,1)}, u32[]{:S(2)}) copy-start(bf16[3072,512]{1,0:T(8,128)(2,1)} %all-gather.2.cloned.1.call-done) | copy-start | bytes 9437188
Sparse Core Ops, SparseCore 0:
  15.1 64.8 reduce-scatter.2
  82.4 23.3 reduce-scatter.4
Sparse Core Ops, SparseCore 1:
  18.3 75.6 all-gather.1
where the time goes:
time: 115 us
  waiting for transfers between devices  84.7 us (74%)
  between operations  15.5 us (13%)
  matrix products  7.91 us (7%)
  other arithmetic  5.14 us (4%)
  local copies, waits for them, and re-layouts  1.37 us (1%)
    reduce_scatter x1, waiting for transfers between devices, per_device(): lax.psum_scatter(grad_term, 'node', scatter_dimension=0, tiled=True)  64.4 us
    all_gather x1, waiting for transfers between devices, per_device(): shard_rows = lax.all_gather(weights, ('node', 'local'), axis=0, tiled=True)  14 us
    reduce_scatter x1, waiting for transfers between devices, per_device(): summed = lax.psum_scatter(across, 'local', scatter_dimension=0, tiled=True)  5.8 us
    dot_general x1, matrix products, per_device(): lax.dot_general(out_grad, shard_rows, contract_cols, preferred_element_ty...  4.22 us
    convert_element_type x1, other arithmetic, per_device(): grad_term = lax.optimization_barrier(grad_term).astype(jnp.float32)  3.56 us
  transfers between devices with their start and end apart: 3, of which 3 were waited for; matrix products, arithmetic and copies ran while one was open for 5% of the time, Pallas kernels for 0%

commit v1 on v0

v1 whole, which is shorter than its diff:
```python
import functools

import jax
import jax.numpy as jnp
from jax import lax
from jax.experimental import pallas as pl
from jax.experimental.pallas import tpu as pltpu
from jax.sharding import PartitionSpec as P

ROWS_ROWS = (((0,), (0,)), ((), ()))
COLS_COLS = (((1,), (1,)), ((), ()))
MESH = pl.DeviceIdType.MESH


def kernel(scale, tok_h, og_h, w_h, proj_o, ig_h, wg_o,
           tok, og, tsib, osib, wf, acc, ig,
           g1b, g2a, g3, sA, sB, rA, rB, s2, r2, zs, zr,
           lsem, ssem, rsem, osem):
    f32, bf16 = jnp.float32, jnp.bfloat16
    node, z = lax.axis_index("node"), lax.axis_index("local")
    c = node % 2
    x = (node // 2) % 2
    y = node // 4
    rows, width = w_h.shape
    group = 4 * rows
    half = width // 2
    nx = node + 2 - 4 * x
    ny = node + 4 - 8 * y
    nd = nx + 4 - 8 * y
    sib = 1 - 2 * c
    dev_x, dev_y, dev_c = (nx, z), (ny, z), (node + sib, z)
    dev_z = [None] + [(node, (z + k) % 4) for k in (1, 2, 3)]
    quad = (node, nx, ny, nd)
    zq = [z] + [(z - k + 4) % 4 for k in (1, 2, 3)]

    def cols(n):
        return pl.ds(pl.multiple_of(n * group, 128), group)

    loads = [
        pltpu.make_async_copy(w_h, wf.at[node, z], lsem.at[0]),
        pltpu.make_async_copy(og_h, og, lsem.at[1]),
        pltpu.make_async_copy(tok_h, tok, lsem.at[2]),
    ]
    for load in loads:
        load.start()

    count = [0]
    started = []

    def remote(src, dst, device):
        i = count[0]
        count[0] += 1
        copy = pltpu.make_async_remote_copy(
            src_ref=src, dst_ref=dst, send_sem=ssem.at[i], recv_sem=rsem.at[i],
            device_id=device, device_id_type=MESH)
        started.append(copy)
        return copy

    barrier = pltpu.get_barrier_semaphore()
    for device in (dev_x, dev_y, dev_c, dev_z[1], dev_z[2], dev_z[3]):
        pl.semaphore_signal(barrier, inc=1, device_id=device, device_id_type=MESH)
    pl.semaphore_wait(barrier, 6)

    og_x = remote(og_h, osib, dev_c)
    og_x.start()
    order = (nd, nx, ny, node)
    tok_x = [remote(tok_h.at[:, cols(n + sib)], tsib.at[i], dev_c) for i, n in enumerate(order)]
    tok_x[0].start()
    wz = {k: remote(w_h, wf.at[node, z], dev_z[k]) for k in (1, 3, 2)}
    for k in (1, 3, 2):
        wz[k].start()
    for i in (1, 2, 3):
        tok_x[i].start()

    def spot(q, r):
        return wf.at[quad[q], zq[r]]

    wx, wy, wd, wc = {}, {}, {}, {}

    def to_sibling(q, r):
        wc[q, r] = remote(spot(q, r), spot(q, r), dev_c)
        wc[q, r].start()

    def send_own(r):
        wx[r] = remote(spot(0, r), spot(0, r), dev_x)
        wx[r].start()
        wy[r] = remote(spot(0, r), spot(0, r), dev_y)
        wy[r].start()
        to_sibling(0, r)

    loads[0].wait()
    send_own(0)

    def grad(i):
        part = lax.dot_general(tok[:, cols(order[i])], og[...], ROWS_ROWS, preferred_element_type=f32)
        part += lax.dot_general(tsib[i], osib[...], ROWS_ROWS, preferred_element_type=f32)
        return part * scale

    loads[1].wait()
    loads[2].wait()
    og_x.wait_recv()

    a1 = [remote(sA.at[i], rA.at[i], dev_x) for i in (0, 1)]
    b1 = [remote(sB.at[i], rB.at[i], dev_y) for i in (0, 1)]
    tok_x[0].wait_recv()
    g = grad(0)
    sA[0] = g[:, :half].astype(bf16)
    a1[0].start()
    sB[0] = g[:, half:].astype(bf16)
    b1[0].start()
    tok_x[1].wait_recv()
    g = grad(1)
    sA[1] = g[:, :half].astype(bf16)
    a1[1].start()
    g1b[...] = g[:, half:]
    tok_x[2].wait_recv()
    g = grad(2)
    sB[1] = g[:, half:].astype(bf16)
    b1[1].start()
    g2a[...] = g[:, :half]
    tok_x[3].wait_recv()
    g3[...] = grad(3)

    for k in (1, 3, 2):
        wz[k].wait_recv()
        send_own(k)

    def relay(r):
        wx[r].wait_recv()
        if r % 2 == 0:
            wd[r] = remote(spot(1, r), spot(1, r), dev_y)
            wd[r].start()
        to_sibling(1, r)
        wy[r].wait_recv()
        if r % 2 == 1:
            wd[r] = remote(spot(2, r), spot(2, r), dev_x)
            wd[r].start()
        to_sibling(2, r)

    relay(0)

    a2 = remote(s2.at[0], r2.at[0], dev_y)
    b2 = remote(s2.at[1], r2.at[1], dev_x)
    a1[0].wait_recv()
    s2[0] = (g2a[...] + rA[0].astype(f32)).astype(bf16)
    a2.start()
    b1[0].wait_recv()
    s2[1] = (g1b[...] + rB[0].astype(f32)).astype(bf16)
    b2.start()

    stores = []

    def use(n, first=False):
        w = wf[n].reshape(group, width)
        part = jnp.dot(tok[:, cols(n)], w, preferred_element_type=f32)
        if first:
            acc[...] = part
        else:
            acc[...] += part
        i = len(stores)
        ig[i] = lax.dot_general(og[...], w, COLS_COLS, preferred_element_type=f32).astype(bf16)
        store = pltpu.make_async_copy(ig.at[i], ig_h.at[:, cols(n)], osem.at[i])
        store.start()
        stores.append(store)

    def use_sibling(q):
        for r in range(4):
            wc[q, r].wait_recv()
        use(quad[q] + sib)

    use(node, True)
    a1[1].wait_recv()
    g3[:, :half] += rA[1].astype(f32)
    b1[1].wait_recv()
    g3[:, half:] += rB[1].astype(f32)

    relay(1)
    use_sibling(0)

    a2.wait_recv()
    g3[:, :half] += r2[0].astype(f32)
    b2.wait_recv()
    g3[:, half:] += r2[1].astype(f32)
    zs[...] = g3[...].astype(bf16).reshape(4, rows, width)
    gz = {}
    for k in (1, 3, 2):
        gz[k] = remote(zs.at[(z + k) % 4], zr.at[k - 1], dev_z[k])
        gz[k].start()

    relay(3)
    relay(2)
    for r in (0, 1, 3, 2):
        wd[r].wait_recv()
        to_sibling(3, r)
    use(nx)
    use(ny)
    use_sibling(1)
    use_sibling(2)

    for k in (1, 3, 2):
        gz[k].wait_recv()
    own = g3[pl.ds(pl.multiple_of(z * rows, 16), rows), :]
    wg_o[...] = (own + zr[0].astype(f32) + zr[1].astype(f32) + zr[2].astype(f32)).astype(bf16)

    use(nd)
    use_sibling(3)
    proj_o[...] = acc[...].astype(bf16)

    for copy in started:
        copy.wait_send()
    for store in stores:
        store.wait()


COPIES = 1 + 4 + 3 + 4 + 4 + 4 + 16 + 4 + 2 + 3


def fused(tokens, out_grad, weights):
    toks, features = tokens.shape
    rows, width = weights.shape
    devices = lax.axis_size("node") * lax.axis_size("local")
    scale = 1.0 / float(toks * devices) ** 0.5
    group, half = 4 * rows, width // 2
    bf16, f32 = jnp.bfloat16, jnp.float32
    return pl.pallas_call(
        functools.partial(kernel, scale),
        out_shape=(
            jax.ShapeDtypeStruct((toks, width), bf16),
            jax.ShapeDtypeStruct((toks, features), bf16),
            jax.ShapeDtypeStruct((rows, width), bf16),
        ),
        in_specs=[pl.BlockSpec(memory_space=pl.ANY)] * 3,
        out_specs=(
            pl.BlockSpec(memory_space=pltpu.VMEM),
            pl.BlockSpec(memory_space=pl.ANY),
            pl.BlockSpec(memory_space=pltpu.VMEM),
        ),
        scratch_shapes=[
            pltpu.VMEM((toks, features), bf16),
            pltpu.VMEM((toks, width), bf16),
            pltpu.VMEM((4, toks, group), bf16),
            pltpu.VMEM((toks, width), bf16),
            pltpu.VMEM((8, 4, rows, width), bf16),
            pltpu.VMEM((toks, width), f32),
            pltpu.VMEM((8, toks, group), bf16),
            pltpu.VMEM((group, half), f32),
            pltpu.VMEM((group, half), f32),
            pltpu.VMEM((group, width), f32),
            pltpu.VMEM((2, group, half), bf16),
            pltpu.VMEM((2, group, half), bf16),
            pltpu.VMEM((2, group, half), bf16),
            pltpu.VMEM((2, group, half), bf16),
            pltpu.VMEM((2, group, half), bf16),
            pltpu.VMEM((2, group, half), bf16),
            pltpu.VMEM((4, rows, width), bf16),
            pltpu.VMEM((3, rows, width), bf16),
            pltpu.SemaphoreType.DMA((3,)),
            pltpu.SemaphoreType.DMA((COPIES,)),
            pltpu.SemaphoreType.DMA((COPIES,)),
            pltpu.SemaphoreType.DMA((8,)),
        ],
        compiler_params=pltpu.CompilerParams(
            collective_id=0, has_side_effects=True, vmem_limit_bytes=40 * 2**20),
        cost_estimate=pl.CostEstimate(
            flops=6 * toks * features * width, bytes_accessed=2 * toks * features * 4, transcendentals=0),
    )(tokens, out_grad, weights)


def plain(tokens, out_grad, weights):
    tok_rows = tokens.shape[0]
    devices = lax.axis_size("node") * lax.axis_size("local")
    grad_scale = 1.0 / jnp.sqrt(jnp.float32(tok_rows * devices))
    grad_term = lax.dot_general(tokens, out_grad, ROWS_ROWS, preferred_element_type=jnp.float32)
    grad_term = (grad_term * grad_scale).astype(jnp.bfloat16)
    grad_term = lax.optimization_barrier(grad_term).astype(jnp.float32)
    shard_rows = lax.all_gather(weights, ("node", "local"), axis=0, tiled=True)
    projected = jnp.dot(tokens, shard_rows, preferred_element_type=jnp.float32).astype(jnp.bfloat16)
    input_grad = lax.dot_general(
        out_grad, shard_rows, COLS_COLS, preferred_element_type=jnp.float32).astype(jnp.bfloat16)
    across = lax.psum_scatter(grad_term, "node", scatter_dimension=0, tiled=True)
    summed = lax.psum_scatter(across, "local", scatter_dimension=0, tiled=True)
    return projected, input_grad, summed.astype(jnp.bfloat16)


def solution(mesh):
    spec = P(("node", "local"), None)
    fits = mesh.shape["node"] == 8 and mesh.shape["local"] == 4
    return jax.shard_map(
        fused if fits else plain,
        mesh=mesh,
        in_specs=(spec, spec, spec),
        out_specs=(spec, spec, spec),
        check_vma=False,
    )
```

time: 115 us -> 49.1 us (0.43)
  waiting for transfers between devices: 84.7 us -> 0 us
  Pallas kernels: 0 us -> 42.5 us
  between operations: 15.5 us -> 0.65 us
  matrix products: 7.91 us -> 0 us
  other arithmetic: 5.14 us -> 0 us
  local copies, waits for them, and re-layouts: 1.37 us -> 5.73 us
    reduce_scatter x2 -> x0, waiting for transfers between devices: 70.2 us -> none  [the longest x1 64.4 us: per_device(): lax.psum_scatter(grad_term, 'node', scatter_dimension=0, tiled=True)]
    pallas_call x0 -> x1, Pallas kernels: none -> 42.5 us  [fused(): pl.pallas_call(functools.partial(kernel, scale), out_shape=(jax.ShapeDtyp...]
    all_gather x1 -> x0, waiting for transfers between devices: 14 us -> none  [per_device(): shard_rows = lax.all_gather(weights, ('node', 'local'), axis=0, tiled=True)]
    dot_general x3 -> x0, matrix products: 7.91 us -> none  [the longest x1 4.22 us: per_device(): lax.dot_general(out_grad, shard_rows, contract_cols, preferred_element_ty...]
    convert_element_type x2 -> x0, other arithmetic: 5.14 us -> none  [the longest x1 3.56 us: per_device(): grad_term = lax.optimization_barrier(grad_term).astype(jnp.float32)]
    unnamed x6 -> x9, local copies, waits for them, and re-layouts: 1.37 us -> 5.73 us
  transfers between devices with their start and end apart: 3 -> 0, of which waited for: 3 -> 0; matrix products, arithmetic and copies ran while one was open for 5% -> 0% of each run, Pallas kernels for 0% -> 0%
where the time goes in v1:
time: 49.1 us; the launch traced here: 48.9 us
  Pallas kernels  42.5 us (87%)
  local copies, waits for them, and re-layouts  5.73 us (12%)
  between operations  0.65 us (1%)
    pallas_call x1, Pallas kernels, fused(): pl.pallas_call(functools.partial(kernel, scale), out_shape=(jax.ShapeDtyp...  42.5 us
    unnamed x9, local copies, waits for them, and re-layouts  5.73 us

profile of v1, /device:TPU:0, one launch (start us, length us, event | category | flops | bytes accessed | tf_op | source)
XLA Modules:
  0.0 48.9 jit_solution(16110427675138461656)
XLA Ops:
  0.6 0.0 copy-start
  0.6 1.4 %copy-done = bf16[256,3072]{1,0:T(8,128)(2,1)S(1)} copy-done((bf16[256,3072]{1,0:T(8,128)(2,1)S(1)}, bf16[256,3072]{1,0:T(8,128)(2,1)}, u32[]{:S(2)}) %copy-start) | copy-done | bytes 1572888
  2.0 0.0 copy-start.1
  2.0 0.9 %copy-done.1 = bf16[256,512]{1,0:T(8,128)(2,1)S(1)} copy-done((bf16[256,512]{1,0:T(8,128)(2,1)S(1)}, bf16[256,512]{1,0:T(8,128)(2,1)}, u32[]{:S(2)}) %copy-start.1) | copy-done | bytes 262168
  3.0 0.0 copy-start.2
  3.0 0.9 %copy-done.2 = bf16[96,512]{1,0:T(8,128)(2,1)S(1)} copy-done((bf16[96,512]{1,0:T(8,128)(2,1)S(1)}, bf16[96,512]{1,0:T(8,128)(2,1)}, u32[]{:S(2)}) %copy-start.2) | copy-done | bytes 98328
  3.9 42.5 %shard_map.58 = (bf16[256,512]{1,0:T(8,128)(2,1)S(1)}, bf16[256,3072]{1,0:T(8,128)(2,1)S(1)}, bf16[96,512]{1,0:T(8,128)(2,1)S(1)}) custom-call(bf16[256,3072]{1,0:T(8,128)(2,1)S(1)} %copy-done, bf16[256,512]{1,0:T(8,128)(2,1)S(1)} %copy-done.1, bf16[96,512]{1,0:T(8,128)(2,1)S(1)} %copy-done.2), custom_call_target="tpu_custom_call" | custom-call | flops 2415919104 | bytes 6291456 | tf_op jit(solution)/shard_map/pallas_call | solution.py:225
  46.4 0.7 %copy.9 = bf16[256,512]{1,0:T(8,128)(2,1)} copy(bf16[256,512]{1,0:T(8,128)(2,1)S(1)} %get-tuple-element.6) | data formatting | bytes 524288
  47.1 1.1 %copy.10 = bf16[256,3072]{1,0:T(8,128)(2,1)} copy(bf16[256,3072]{1,0:T(8,128)(2,1)S(1)} %get-tuple-element.7) | data formatting | bytes 3145728
  48.3 0.6 %copy.11 = bf16[96,512]{1,0:T(8,128)(2,1)} copy(bf16[96,512]{1,0:T(8,128)(2,1)S(1)} %get-tuple-element.8) | data formatting | bytes 196608
Async XLA Ops:
  0.6 1.4 %copy-start = (bf16[256,3072]{1,0:T(8,128)(2,1)S(1)}, bf16[256,3072]{1,0:T(8,128)(2,1)}, u32[]{:S(2)}) copy-start(bf16[256,3072]{1,0:T(8,128)(2,1)} %tok_h.1) | copy-start | bytes 4718596
  2.0 0.9 %copy-start.1 = (bf16[256,512]{1,0:T(8,128)(2,1)S(1)}, bf16[256,512]{1,0:T(8,128)(2,1)}, u32[]{:S(2)}) copy-start(bf16[256,512]{1,0:T(8,128)(2,1)} %og_h.1) | copy-start | bytes 786436
  3.0 0.9 %copy-start.2 = (bf16[96,512]{1,0:T(8,128)(2,1)S(1)}, bf16[96,512]{1,0:T(8,128)(2,1)}, u32[]{:S(2)}) copy-start(bf16[96,512]{1,0:T(8,128)(2,1)} %w_h.1) | copy-start | bytes 294916

commit v2 on v1

--- a/solution.py
+++ b/solution.py
@@ -121,10 +121,6 @@
     tok_x[3].wait_recv()
     g3[...] = grad(3)
 
-    for k in (1, 3, 2):
-        wz[k].wait_recv()
-        send_own(k)
-
     def relay(r):
         wx[r].wait_recv()
         if r % 2 == 0:
@@ -137,8 +133,6 @@
             wd[r].start()
         to_sibling(2, r)
 
-    relay(0)
-
     a2 = remote(s2.at[0], r2.at[0], dev_y)
     b2 = remote(s2.at[1], r2.at[1], dev_x)
     a1[0].wait_recv()
@@ -147,6 +141,12 @@
     b1[0].wait_recv()
     s2[1] = (g1b[...] + rB[0].astype(f32)).astype(bf16)
     b2.start()
+
+    for k in (1, 3, 2):
+        wz[k].wait_recv()
+        send_own(k)
+
+    relay(0)
 
     stores = []
 
@@ -168,14 +168,10 @@
             wc[q, r].wait_recv()
         use(quad[q] + sib)
 
-    use(node, True)
     a1[1].wait_recv()
     g3[:, :half] += rA[1].astype(f32)
     b1[1].wait_recv()
     g3[:, half:] += rB[1].astype(f32)
-
-    relay(1)
-    use_sibling(0)
 
     a2.wait_recv()
     g3[:, :half] += r2[0].astype(f32)
@@ -187,8 +183,11 @@
         gz[k] = remote(zs.at[(z + k) % 4], zr.at[k - 1], dev_z[k])
         gz[k].start()
 
+    relay(1)
     relay(3)
     relay(2)
+    use(node, True)
+    use_sibling(0)
     for r in (0, 1, 3, 2):
         wd[r].wait_recv()
         to_sibling(3, r)
@@ -229,7 +228,7 @@
             jax.ShapeDtypeStruct((toks, features), bf16),
             jax.ShapeDtypeStruct((rows, width), bf16),
         ),
-        in_specs=[pl.BlockSpec(memory_space=pl.ANY)] * 3,
+        in_specs=[pl.BlockSpec(memory_space=pltpu.HBM)] * 3,
         out_specs=(
             pl.BlockSpec(memory_space=pltpu.VMEM),
             pl.BlockSpec(memory_space=pl.ANY),

time: 49.1 us -> 43.9 us (0.89)
  Pallas kernels: 42.5 us -> 37.3 us
    pallas_call x1, Pallas kernels: 42.5 us -> 37.3 us  [fused(): pl.pallas_call(functools.partial(kernel, scale), out_shape=(jax.ShapeDtyp...]
where the time goes in v2:
time: 43.9 us; the launch traced here: 43.7 us
  Pallas kernels  37.3 us (85%)
  local copies, waits for them, and re-layouts  5.73 us (13%)
  between operations  0.65 us (1%)
    pallas_call x1, Pallas kernels, fused(): pl.pallas_call(functools.partial(kernel, scale), out_shape=(jax.ShapeDtyp...  37.3 us
    unnamed x9, local copies, waits for them, and re-layouts  5.73 us

profile of v2, /device:TPU:0, one launch (start us, length us, event | category | flops | bytes accessed | tf_op | source)
XLA Modules:
  0.0 43.7 jit_solution(13514019886423595274)
XLA Ops:
  0.6 0.0 copy-start
  0.6 1.4 %copy-done = bf16[256,3072]{1,0:T(8,128)(2,1)S(1)} copy-done((bf16[256,3072]{1,0:T(8,128)(2,1)S(1)}, bf16[256,3072]{1,0:T(8,128)(2,1)}, u32[]{:S(2)}) %copy-start) | copy-done | bytes 1572888
  2.0 0.0 copy-start.1
  2.0 0.9 %copy-done.1 = bf16[256,512]{1,0:T(8,128)(2,1)S(1)} copy-done((bf16[256,512]{1,0:T(8,128)(2,1)S(1)}, bf16[256,512]{1,0:T(8,128)(2,1)}, u32[]{:S(2)}) %copy-start.1) | copy-done | bytes 262168
  3.0 0.0 copy-start.2
  3.0 0.9 %copy-done.2 = bf16[96,512]{1,0:T(8,128)(2,1)S(1)} copy-done((bf16[96,512]{1,0:T(8,128)(2,1)S(1)}, bf16[96,512]{1,0:T(8,128)(2,1)}, u32[]{:S(2)}) %copy-start.2) | copy-done | bytes 98328
  3.9 37.3 %shard_map.58 = (bf16[256,512]{1,0:T(8,128)(2,1)S(1)}, bf16[256,3072]{1,0:T(8,128)(2,1)S(1)}, bf16[96,512]{1,0:T(8,128)(2,1)S(1)}) custom-call(bf16[256,3072]{1,0:T(8,128)(2,1)S(1)} %copy-done, bf16[256,512]{1,0:T(8,128)(2,1)S(1)} %copy-done.1, bf16[96,512]{1,0:T(8,128)(2,1)S(1)} %copy-done.2), custom_call_target="tpu_custom_call" | custom-call | flops 2415919104 | bytes 6291456 | tf_op jit(solution)/shard_map/pallas_call | solution.py:224
  41.2 0.7 %copy.9 = bf16[256,512]{1,0:T(8,128)(2,1)} copy(bf16[256,512]{1,0:T(8,128)(2,1)S(1)} %get-tuple-element.6) | data formatting | bytes 524288
  41.9 1.1 %copy.10 = bf16[256,3072]{1,0:T(8,128)(2,1)} copy(bf16[256,3072]{1,0:T(8,128)(2,1)S(1)} %get-tuple-element.7) | data formatting | bytes 3145728
  43.0 0.6 %copy.11 = bf16[96,512]{1,0:T(8,128)(2,1)} copy(bf16[96,512]{1,0:T(8,128)(2,1)S(1)} %get-tuple-element.8) | data formatting | bytes 196608
Async XLA Ops:
  0.6 1.4 %copy-start = (bf16[256,3072]{1,0:T(8,128)(2,1)S(1)}, bf16[256,3072]{1,0:T(8,128)(2,1)}, u32[]{:S(2)}) copy-start(bf16[256,3072]{1,0:T(8,128)(2,1)} %tok_h.1) | copy-start | bytes 4718596
  2.0 0.9 %copy-start.1 = (bf16[256,512]{1,0:T(8,128)(2,1)S(1)}, bf16[256,512]{1,0:T(8,128)(2,1)}, u32[]{:S(2)}) copy-start(bf16[256,512]{1,0:T(8,128)(2,1)} %og_h.1) | copy-start | bytes 786436
  3.0 0.9 %copy-start.2 = (bf16[96,512]{1,0:T(8,128)(2,1)S(1)}, bf16[96,512]{1,0:T(8,128)(2,1)}, u32[]{:S(2)}) copy-start(bf16[96,512]{1,0:T(8,128)(2,1)} %w_h.1) | copy-start | bytes 294916

commit v3 on v2

--- a/solution.py
+++ b/solution.py
@@ -96,6 +96,34 @@
         part += lax.dot_general(tsib[i], osib[...], ROWS_ROWS, preferred_element_type=f32)
         return part * scale
 
+    def relay(r):
+        wx[r].wait_recv()
+        to_sibling(1, r)
+        wy[r].wait_recv()
+        to_sibling(2, r)
+
+    def diagonal():
+        low, high = pl.ds(0, rows // 2), pl.ds(rows // 2, rows // 2)
+        wx[0].wait_recv()
+        part = wf.at[nx, z, low]
+        d_low = remote(part, part, dev_y)
+        d_low.start()
+        wy[0].wait_recv()
+        part = wf.at[ny, z, high]
+        d_high = remote(part, part, dev_x)
+        d_high.start()
+        return d_low, d_high
+
+    def diagonal_along_z():
+        d_low.wait_recv()
+        d_high.wait_recv()
+        for k in (1, 3, 2):
+            wd[k] = remote(spot(3, 0), spot(3, 0), dev_z[k])
+            wd[k].start()
+        to_sibling(1, 0)
+        to_sibling(2, 0)
+        to_sibling(3, 0)
+
     loads[1].wait()
     loads[2].wait()
     og_x.wait_recv()
@@ -108,6 +136,7 @@
     a1[0].start()
     sB[0] = g[:, half:].astype(bf16)
     b1[0].start()
+    d_low, d_high = diagonal()
     tok_x[1].wait_recv()
     g = grad(1)
     sA[1] = g[:, :half].astype(bf16)
@@ -121,18 +150,6 @@
     tok_x[3].wait_recv()
     g3[...] = grad(3)
 
-    def relay(r):
-        wx[r].wait_recv()
-        if r % 2 == 0:
-            wd[r] = remote(spot(1, r), spot(1, r), dev_y)
-            wd[r].start()
-        to_sibling(1, r)
-        wy[r].wait_recv()
-        if r % 2 == 1:
-            wd[r] = remote(spot(2, r), spot(2, r), dev_x)
-            wd[r].start()
-        to_sibling(2, r)
-
     a2 = remote(s2.at[0], r2.at[0], dev_y)
     b2 = remote(s2.at[1], r2.at[1], dev_x)
     a1[0].wait_recv()
@@ -145,8 +162,8 @@
     for k in (1, 3, 2):
         wz[k].wait_recv()
         send_own(k)
-
-    relay(0)
+    diagonal_along_z()
+
 
     stores = []
 
@@ -188,7 +205,7 @@
     relay(2)
     use(node, True)
     use_sibling(0)
-    for r in (0, 1, 3, 2):
+    for r in (1, 3, 2):
         wd[r].wait_recv()
         to_sibling(3, r)
     use(nx)
@@ -211,7 +228,16 @@
         store.wait()
 
 
-COPIES = 1 + 4 + 3 + 4 + 4 + 4 + 16 + 4 + 2 + 3
+def hand_on(a, b, c, a_out, b_out, c_out, sem):
+    pairs = ((a, a_out), (b, b_out), (c, c_out))
+    copies = [pltpu.make_async_copy(src, dst, sem.at[i]) for i, (src, dst) in enumerate(pairs)]
+    for copy in copies:
+        copy.start()
+    for copy in copies:
+        copy.wait()
+
+
+COPIES = 1 + 4 + 3 + 4 + 4 + 5 + 16 + 4 + 2 + 3
 
 
 def fused(tokens, out_grad, weights):
@@ -221,7 +247,7 @@
     scale = 1.0 / float(toks * devices) ** 0.5
     group, half = 4 * rows, width // 2
     bf16, f32 = jnp.bfloat16, jnp.float32
-    return pl.pallas_call(
+    results = pl.pallas_call(
         functools.partial(kernel, scale),
         out_shape=(
             jax.ShapeDtypeStruct((toks, width), bf16),
@@ -263,6 +289,14 @@
         cost_estimate=pl.CostEstimate(
             flops=6 * toks * features * width, bytes_accessed=2 * toks * features * 4, transcendentals=0),
     )(tokens, out_grad, weights)
+    return pl.pallas_call(
+        hand_on,
+        out_shape=tuple(jax.ShapeDtypeStruct(a.shape, a.dtype) for a in results),
+        in_specs=[pl.BlockSpec(memory_space=pl.ANY)] * 3,
+        out_specs=[pl.BlockSpec(memory_space=pl.ANY)] * 3,
+        scratch_shapes=[pltpu.SemaphoreType.DMA((3,))],
+        compiler_params=pltpu.CompilerParams(vmem_limit_bytes=2**20),
+    )(*results)
 
 
 def plain(tokens, out_grad, weights):

time: 43.9 us -> 41.1 us (0.936)
  local copies, waits for them, and re-layouts: 5.73 us -> 3.24 us
    unnamed x9 -> x6, local copies, waits for them, and re-layouts: 5.73 us -> 3.24 us
    pallas_call x1, Pallas kernels: 37.3 us -> 35.7 us  [fused(): pl.pallas_call(functools.partial(kernel, scale), out_shape=(jax.ShapeDtyp...]
    pallas_call x0 -> x1, Pallas kernels: none -> 1.27 us  [fused(): pl.pallas_call(hand_on, out_shape=tuple((jax.ShapeDtypeStruct(a.shape, a....]
where the time goes in v3:
time: 41.1 us; the launch traced here: 40.9 us
  Pallas kernels  37 us (90%)
  local copies, waits for them, and re-layouts  3.24 us (8%)
  between operations  0.65 us (2%)
    pallas_call x1, Pallas kernels, fused(): pl.pallas_call(functools.partial(kernel, scale), out_shape=(jax.ShapeDtyp...  35.7 us
    unnamed x6, local copies, waits for them, and re-layouts  3.24 us
    pallas_call x1, Pallas kernels, fused(): pl.pallas_call(hand_on, out_shape=tuple((jax.ShapeDtypeStruct(a.shape, a....  1.27 us

profile of v3, /device:TPU:0, one launch (start us, length us, event | category | flops | bytes accessed | tf_op | source)
XLA Modules:
  0.0 40.9 jit_solution(5082805955035994745)
XLA Ops:
  0.6 0.0 copy-start
  0.6 1.4 %copy-done = bf16[256,3072]{1,0:T(8,128)(2,1)S(1)} copy-done((bf16[256,3072]{1,0:T(8,128)(2,1)S(1)}, bf16[256,3072]{1,0:T(8,128)(2,1)}, u32[]{:S(2)}) %copy-start) | copy-done | bytes 1572888
  2.0 0.0 copy-start.1
  2.0 0.9 %copy-done.1 = bf16[256,512]{1,0:T(8,128)(2,1)S(1)} copy-done((bf16[256,512]{1,0:T(8,128)(2,1)S(1)}, bf16[256,512]{1,0:T(8,128)(2,1)}, u32[]{:S(2)}) %copy-start.1) | copy-done | bytes 262168
  3.0 0.0 copy-start.2
  3.0 0.9 %copy-done.2 = bf16[96,512]{1,0:T(8,128)(2,1)S(1)} copy-done((bf16[96,512]{1,0:T(8,128)(2,1)S(1)}, bf16[96,512]{1,0:T(8,128)(2,1)}, u32[]{:S(2)}) %copy-start.2) | copy-done | bytes 98328
  3.9 35.7 %shard_map.58 = (bf16[256,512]{1,0:T(8,128)(2,1)S(1)}, bf16[256,3072]{1,0:T(8,128)(2,1)S(1)}, bf16[96,512]{1,0:T(8,128)(2,1)S(1)}) custom-call(bf16[256,3072]{1,0:T(8,128)(2,1)S(1)} %copy-done, bf16[256,512]{1,0:T(8,128)(2,1)S(1)} %copy-done.1, bf16[96,512]{1,0:T(8,128)(2,1)S(1)} %copy-done.2), custom_call_target="tpu_custom_call" | custom-call | flops 2415919104 | bytes 6291456 | tf_op jit(solution)/shard_map/pallas_call | solution.py:250
  39.6 1.3 %shard_map.59 = (bf16[256,512]{1,0:T(8,128)(2,1)}, bf16[256,3072]{1,0:T(8,128)(2,1)}, bf16[96,512]{1,0:T(8,128)(2,1)}) custom-call(bf16[256,512]{1,0:T(8,128)(2,1)S(1)} %get-tuple-element.6.a, bf16[256,3072]{1,0:T(8,128)(2,1)S(1)} %get-tuple-element.7.b, bf16[96,512]{1,0:T(8,128)(2,1)S(1)} %get-tuple-element.8.c), custom_call_target="tpu_custom_call" | custom-call | tf_op jit(solution)/shard_map/pallas_call | solution.py:292
Async XLA Ops:
  0.6 1.4 %copy-start = (bf16[256,3072]{1,0:T(8,128)(2,1)S(1)}, bf16[256,3072]{1,0:T(8,128)(2,1)}, u32[]{:S(2)}) copy-start(bf16[256,3072]{1,0:T(8,128)(2,1)} %tok_h.1) | copy-start | bytes 4718596
  2.0 0.9 %copy-start.1 = (bf16[256,512]{1,0:T(8,128)(2,1)S(1)}, bf16[256,512]{1,0:T(8,128)(2,1)}, u32[]{:S(2)}) copy-start(bf16[256,512]{1,0:T(8,128)(2,1)} %og_h.1) | copy-start | bytes 786436
  3.0 0.9 %copy-start.2 = (bf16[96,512]{1,0:T(8,128)(2,1)S(1)}, bf16[96,512]{1,0:T(8,128)(2,1)}, u32[]{:S(2)}) copy-start(bf16[96,512]{1,0:T(8,128)(2,1)} %w_h.1) | copy-start | bytes 294916

commit v4 on v3

--- a/solution.py
+++ b/solution.py
@@ -24,6 +24,7 @@
     rows, width = w_h.shape
     group = 4 * rows
     half = width // 2
+    quarter = width // 4
     nx = node + 2 - 4 * x
     ny = node + 4 - 8 * y
     nd = nx + 4 - 8 * y
@@ -128,42 +129,79 @@
     loads[2].wait()
     og_x.wait_recv()
 
-    a1 = [remote(sA.at[i], rA.at[i], dev_x) for i in (0, 1)]
-    b1 = [remote(sB.at[i], rB.at[i], dev_y) for i in (0, 1)]
+    a1 = [[remote(sA.at[i, j], rA.at[i, j], dev_x) for j in (0, 1)] for i in (0, 1)]
+    b1 = [[remote(sB.at[i, j], rB.at[i, j], dev_y) for j in (0, 1)] for i in (0, 1)]
+    a2 = [remote(s2.at[0, j], r2.at[0, j], dev_y) for j in (0, 1)]
+    b2 = [remote(s2.at[1, j], r2.at[1, j], dev_x) for j in (0, 1)]
+
+    def left(j):
+        return slice(j * quarter, (j + 1) * quarter)
+
+    def right(j):
+        return slice(half + j * quarter, half + (j + 1) * quarter)
+
     tok_x[0].wait_recv()
     g = grad(0)
-    sA[0] = g[:, :half].astype(bf16)
-    a1[0].start()
-    sB[0] = g[:, half:].astype(bf16)
-    b1[0].start()
+    for j in (0, 1):
+        sA[0, j] = g[:, left(j)].astype(bf16)
+        sB[0, j] = g[:, right(j)].astype(bf16)
+    a1[0][0].start()
+    b1[0][0].start()
     d_low, d_high = diagonal()
     tok_x[1].wait_recv()
     g = grad(1)
-    sA[1] = g[:, :half].astype(bf16)
-    a1[1].start()
-    g1b[...] = g[:, half:]
+    for j in (0, 1):
+        sA[1, j] = g[:, left(j)].astype(bf16)
+        g1b[j] = g[:, right(j)]
+    a1[1][0].start()
     tok_x[2].wait_recv()
     g = grad(2)
-    sB[1] = g[:, half:].astype(bf16)
-    b1[1].start()
-    g2a[...] = g[:, :half]
+    for j in (0, 1):
+        sB[1, j] = g[:, right(j)].astype(bf16)
+        g2a[j] = g[:, left(j)]
+    b1[1][0].start()
+    a1[0][1].start()
+    b1[0][1].start()
     tok_x[3].wait_recv()
-    g3[...] = grad(3)
-
-    a2 = remote(s2.at[0], r2.at[0], dev_y)
-    b2 = remote(s2.at[1], r2.at[1], dev_x)
-    a1[0].wait_recv()
-    s2[0] = (g2a[...] + rA[0].astype(f32)).astype(bf16)
-    a2.start()
-    b1[0].wait_recv()
-    s2[1] = (g1b[...] + rB[0].astype(f32)).astype(bf16)
-    b2.start()
-
-    for k in (1, 3, 2):
-        wz[k].wait_recv()
-        send_own(k)
+    g = grad(3)
+    for j in (0, 1):
+        g3[j, :, :quarter] = g[:, left(j)]
+        g3[j, :, quarter:] = g[:, right(j)]
+
+    def second(j):
+        a1[0][j].wait_recv()
+        s2[0, j] = (g2a[j] + rA[0, j].astype(f32)).astype(bf16)
+        a2[j].start()
+        b1[0][j].wait_recv()
+        s2[1, j] = (g1b[j] + rB[0, j].astype(f32)).astype(bf16)
+        b2[j].start()
+
+    gz = {}
+
+    def along_z(j):
+        a1[1][j].wait_recv()
+        b1[1][j].wait_recv()
+        a2[j].wait_recv()
+        b2[j].wait_recv()
+        g3[j, :, :quarter] += rA[1, j].astype(f32) + r2[0, j].astype(f32)
+        g3[j, :, quarter:] += rB[1, j].astype(f32) + r2[1, j].astype(f32)
+        zs[j] = g3[j].astype(bf16).reshape(4, rows, half)
+        for k in (1, 3, 2):
+            gz[j, k] = remote(zs.at[j, (z + k) % 4], zr.at[j, k - 1], dev_z[k])
+            gz[j, k].start()
+
     diagonal_along_z()
-
+    second(0)
+    a1[1][1].start()
+    b1[1][1].start()
+    second(1)
+    wz[1].wait_recv()
+    send_own(1)
+    wz[3].wait_recv()
+    send_own(3)
+    wz[2].wait_recv()
+    send_own(2)
+    along_z(0)
 
     stores = []
 
@@ -185,20 +223,7 @@
             wc[q, r].wait_recv()
         use(quad[q] + sib)
 
-    a1[1].wait_recv()
-    g3[:, :half] += rA[1].astype(f32)
-    b1[1].wait_recv()
-    g3[:, half:] += rB[1].astype(f32)
-
-    a2.wait_recv()
-    g3[:, :half] += r2[0].astype(f32)
-    b2.wait_recv()
-    g3[:, half:] += r2[1].astype(f32)
-    zs[...] = g3[...].astype(bf16).reshape(4, rows, width)
-    gz = {}
-    for k in (1, 3, 2):
-        gz[k] = remote(zs.at[(z + k) % 4], zr.at[k - 1], dev_z[k])
-        gz[k].start()
+    along_z(1)
 
     relay(1)
     relay(3)
@@ -213,10 +238,13 @@
     use_sibling(1)
     use_sibling(2)
 
-    for k in (1, 3, 2):
-        gz[k].wait_recv()
-    own = g3[pl.ds(pl.multiple_of(z * rows, 16), rows), :]
-    wg_o[...] = (own + zr[0].astype(f32) + zr[1].astype(f32) + zr[2].astype(f32)).astype(bf16)
+    own = pl.ds(pl.multiple_of(z * rows, 16), rows)
+    for j in (0, 1):
+        for k in (1, 3, 2):
+            gz[j, k].wait_recv()
+        total = g3[j, own, :] + zr[j, 0].astype(f32) + zr[j, 1].astype(f32) + zr[j, 2].astype(f32)
+        wg_o[:, left(j)] = total[:, :quarter].astype(bf16)
+        wg_o[:, right(j)] = total[:, quarter:].astype(bf16)
 
     use(nd)
     use_sibling(3)
@@ -237,7 +265,7 @@
         copy.wait()
 
 
-COPIES = 1 + 4 + 3 + 4 + 4 + 5 + 16 + 4 + 2 + 3
+COPIES = 1 + 4 + 3 + 4 + 4 + 5 + 16 + 8 + 4 + 6
 
 
 def fused(tokens, out_grad, weights):
@@ -245,7 +273,7 @@
     rows, width = weights.shape
     devices = lax.axis_size("node") * lax.axis_size("local")
     scale = 1.0 / float(toks * devices) ** 0.5
-    group, half = 4 * rows, width // 2
+    group, half, quarter = 4 * rows, width // 2, width // 4
     bf16, f32 = jnp.bfloat16, jnp.float32
     results = pl.pallas_call(
         functools.partial(kernel, scale),
@@ -268,17 +296,17 @@
             pltpu.VMEM((8, 4, rows, width), bf16),
             pltpu.VMEM((toks, width), f32),
             pltpu.VMEM((8, toks, group), bf16),
-            pltpu.VMEM((group, half), f32),
-            pltpu.VMEM((group, half), f32),
-            pltpu.VMEM((group, width), f32),
-            pltpu.VMEM((2, group, half), bf16),
-            pltpu.VMEM((2, group, half), bf16),
-            pltpu.VMEM((2, group, half), bf16),
-            pltpu.VMEM((2, group, half), bf16),
-            pltpu.VMEM((2, group, half), bf16),
-            pltpu.VMEM((2, group, half), bf16),
-            pltpu.VMEM((4, rows, width), bf16),
-            pltpu.VMEM((3, rows, width), bf16),
+            pltpu.VMEM((2, group, quarter), f32),
+            pltpu.VMEM((2, group, quarter), f32),
+            pltpu.VMEM((2, group, half), f32),
+            pltpu.VMEM((2, 2, group, quarter), bf16),
+            pltpu.VMEM((2, 2, group, quarter), bf16),
+            pltpu.VMEM((2, 2, group, quarter), bf16),
+            pltpu.VMEM((2, 2, group, quarter), bf16),
+            pltpu.VMEM((2, 2, group, quarter), bf16),
+            pltpu.VMEM((2, 2, group, quarter), bf16),
+            pltpu.VMEM((2, 4, rows, half), bf16),
+            pltpu.VMEM((2, 3, rows, half), bf16),
             pltpu.SemaphoreType.DMA((3,)),
             pltpu.SemaphoreType.DMA((COPIES,)),
             pltpu.SemaphoreType.DMA((COPIES,)),

time: 41.1 us -> 40.1 us (0.976)
  Pallas kernels: 37 us -> 36 us
    pallas_call x1, Pallas kernels: 35.7 us -> 34.7 us  [fused(): pl.pallas_call(functools.partial(kernel, scale), out_shape=(jax.ShapeDtyp...]
where the time goes in v4:
time: 40.1 us; the launch traced here: 39.9 us
  Pallas kernels  36 us (90%)
  local copies, waits for them, and re-layouts  3.24 us (8%)
  between operations  0.65 us (2%)
    pallas_call x1, Pallas kernels, fused(): pl.pallas_call(functools.partial(kernel, scale), out_shape=(jax.ShapeDtyp...  34.7 us
    unnamed x6, local copies, waits for them, and re-layouts  3.24 us
    pallas_call x1, Pallas kernels, fused(): pl.pallas_call(hand_on, out_shape=tuple((jax.ShapeDtypeStruct(a.shape, a....  1.27 us

profile of v4, /device:TPU:0, one launch (start us, length us, event | category | flops | bytes accessed | tf_op | source)
XLA Modules:
  0.0 39.9 jit_solution(1055197988946205503)
XLA Ops:
  0.6 0.0 copy-start
  0.6 1.4 %copy-done = bf16[256,3072]{1,0:T(8,128)(2,1)S(1)} copy-done((bf16[256,3072]{1,0:T(8,128)(2,1)S(1)}, bf16[256,3072]{1,0:T(8,128)(2,1)}, u32[]{:S(2)}) %copy-start) | copy-done | bytes 1572888
  2.0 0.0 copy-start.1
  2.0 0.9 %copy-done.1 = bf16[256,512]{1,0:T(8,128)(2,1)S(1)} copy-done((bf16[256,512]{1,0:T(8,128)(2,1)S(1)}, bf16[256,512]{1,0:T(8,128)(2,1)}, u32[]{:S(2)}) %copy-start.1) | copy-done | bytes 262168
  3.0 0.0 copy-start.2
  3.0 0.9 %copy-done.2 = bf16[96,512]{1,0:T(8,128)(2,1)S(1)} copy-done((bf16[96,512]{1,0:T(8,128)(2,1)S(1)}, bf16[96,512]{1,0:T(8,128)(2,1)}, u32[]{:S(2)}) %copy-start.2) | copy-done | bytes 98328
  3.9 34.7 %shard_map.58 = (bf16[256,512]{1,0:T(8,128)(2,1)S(1)}, bf16[256,3072]{1,0:T(8,128)(2,1)S(1)}, bf16[96,512]{1,0:T(8,128)(2,1)S(1)}) custom-call(bf16[256,3072]{1,0:T(8,128)(2,1)S(1)} %copy-done, bf16[256,512]{1,0:T(8,128)(2,1)S(1)} %copy-done.1, bf16[96,512]{1,0:T(8,128)(2,1)S(1)} %copy-done.2), custom_call_target="tpu_custom_call" | custom-call | flops 2415919104 | bytes 6291456 | tf_op jit(solution)/shard_map/pallas_call | solution.py:278
  38.6 1.3 %shard_map.59 = (bf16[256,512]{1,0:T(8,128)(2,1)}, bf16[256,3072]{1,0:T(8,128)(2,1)}, bf16[96,512]{1,0:T(8,128)(2,1)}) custom-call(bf16[256,512]{1,0:T(8,128)(2,1)S(1)} %get-tuple-element.6.a, bf16[256,3072]{1,0:T(8,128)(2,1)S(1)} %get-tuple-element.7.b, bf16[96,512]{1,0:T(8,128)(2,1)S(1)} %get-tuple-element.8.c), custom_call_target="tpu_custom_call" | custom-call | tf_op jit(solution)/shard_map/pallas_call | solution.py:320
Async XLA Ops:
  0.6 1.4 %copy-start = (bf16[256,3072]{1,0:T(8,128)(2,1)S(1)}, bf16[256,3072]{1,0:T(8,128)(2,1)}, u32[]{:S(2)}) copy-start(bf16[256,3072]{1,0:T(8,128)(2,1)} %tok_h.1) | copy-start | bytes 4718596
  2.0 0.9 %copy-start.1 = (bf16[256,512]{1,0:T(8,128)(2,1)S(1)}, bf16[256,512]{1,0:T(8,128)(2,1)}, u32[]{:S(2)}) copy-start(bf16[256,512]{1,0:T(8,128)(2,1)} %og_h.1) | copy-start | bytes 786436
  3.0 0.9 %copy-start.2 = (bf16[96,512]{1,0:T(8,128)(2,1)S(1)}, bf16[96,512]{1,0:T(8,128)(2,1)}, u32[]{:S(2)}) copy-start(bf16[96,512]{1,0:T(8,128)(2,1)} %w_h.1) | copy-start | bytes 294916
